TPU v7x, 32 devices: a whole 2x2x4 slice. The times are simulated.
32 devices in a mesh: parts: 2 (over y), blk: 16 (over z, x, core).
Axes of the slice: x: 2, y: 2, z: 4, core: 2. Of those that a mesh axis runs over, the one named last changes fastest.
Arguments:
- embedding: float32 [16384, 768], P(('parts', 'blk')), parts along dimension 0
- row_owner: int32 [16384], P(('parts', 'blk')), parts along dimension 0, may hold values from 0 to 15, as said below
- cluster_id: int32 [16384], P(('parts', 'blk')), parts along dimension 0, may hold values from 0 to 63, as said below
Outputs:
- nearest: float32 [16384], P(('parts', 'blk')), parts along dimension 0
There are 2 independent parts, one for each index of `parts`. A program takes and returns all parts, laid end to end along the dimension named above; each array names one. Nothing has to cross between parts.
Inputs may be any that keep to these rules, and one draw needn't show every extreme that they name: Among the 512 rows of one blk device at most 64 have the same owner, and some owner gets exactly 64; row_owner // 4 equals cluster_id // 16. cluster_id // 16 is the owner group of the cluster.
All inputs are finite; a program needn't handle non-finite values.
Results may differ from a plain program's by a relative error of at most 0.0003.
Values may be sent and summed in bfloat16 or wider, within the bound.
No kernel may reach another device: no remote copies, remote signals or barrier semaphores. Data moves between devices by JAX's collectives and lax.ppermute only.
A program may use at most 64 MiB of HBM per device.

v0:
```python
import jax
import jax.numpy as jnp
from jax import lax
from jax.sharding import PartitionSpec as P

GROUP = 4


def from_partner(array, axis, distance):
    return lax.ppermute(array, axis, [(i, i ^ 1 << distance) for i in range(lax.axis_size(axis))])


def compare(best, q_vec, q_label, k_vec, k_label, itself):
    scores = jnp.einsum("qd,kd->qk", q_vec, k_vec, preferred_element_type=jnp.float32)
    allowed = (q_label[:, None] == k_label[None, :]) & (k_label[None, :] >= 0)
    diagonal = jnp.arange(q_vec.shape[0])[:, None] == jnp.arange(k_vec.shape[0])[None, :]
    allowed = allowed & jnp.logical_not(diagonal & itself)
    return jnp.maximum(best, jnp.max(jnp.where(allowed, scores, jnp.float32(-1.0)), axis=1))


def on_device(embedding, row_owner, cluster_id):
    rows, width = embedding.shape
    devices = lax.axis_size("blk")
    capacity = max(2, 2 * rows // devices)
    slots = devices * capacity
    squares = jnp.sum(embedding * embedding, axis=1, keepdims=True)
    unit = (embedding * lax.rsqrt(squares + 1e-06)).astype(jnp.bfloat16)
    same_owner = row_owner[:, None] == row_owner[None, :]
    before = jnp.arange(rows)[None, :] < jnp.arange(rows)[:, None]
    rank = jnp.sum((same_owner & before).astype(jnp.int32), axis=1)
    slot = row_owner * capacity + rank
    slot_hot = slot[:, None] == jnp.arange(slots)[None, :]
    send_vec = jnp.dot(
        slot_hot.astype(jnp.bfloat16).T, unit, preferred_element_type=jnp.float32
    ).astype(jnp.bfloat16)
    label_sum = jnp.dot(
        slot_hot.astype(jnp.float32).T,
        (cluster_id + 1).astype(jnp.float32),
        precision=lax.Precision.HIGHEST,
    )
    send_label = label_sum.astype(jnp.int32) - 1
    best = jnp.full((slots,), -1.0, jnp.float32)
    got_vec, got_label = (
        lax.all_to_all(
            send_vec.reshape(devices, capacity, width),
            "blk",
            split_axis=0,
            concat_axis=0,
            tiled=True,
        ),
        lax.all_to_all(
            send_label.reshape(devices, capacity), "blk", split_axis=0, concat_axis=0, tiled=True
        ),
    )
    q_vec = got_vec.reshape(slots, width)
    q_label = got_label.reshape(slots)
    best = compare(best, q_vec, q_label, q_vec, q_label, True)
    held_vec, held_label = (q_vec, q_label)
    for bit in range(GROUP.bit_length() - 1):
        other_vec, other_label = from_partner((held_vec, held_label), "blk", bit)
        best = compare(best, q_vec, q_label, other_vec, other_label, False)
        held_vec = jnp.concatenate([held_vec, other_vec], axis=0)
        held_label = jnp.concatenate([held_label, other_label], axis=0)
    back = lax.all_to_all(
        best.reshape(devices, capacity), "blk", split_axis=0, concat_axis=0, tiled=True
    )
    return jnp.dot(
        slot_hot.astype(jnp.float32), back.reshape(slots), precision=lax.Precision.HIGHEST
    )


def solution(mesh):
    placed = (P(("parts", "blk"), None), P(("parts", "blk")), P(("parts", "blk")))
    return jax.shard_map(
        on_device, mesh=mesh, in_specs=placed, out_specs=P(("parts", "blk")), check_vma=False
    )
```

profile of v0, /device:TPU:0, one launch (start us, length us, event | category | flops | bytes accessed | tf_op | source)
XLA Modules:
  0.0 156.5 jit_solution(2976201385593134318)
XLA Ops:
  0.0 1.6 %multiply_reduce_fusion = f32[512]{0:T(512)S(1)} fusion(f32[512,768]{1,0:T(8,128)} %param.3), kind=kLoop, calls=%fused_computation.14 | loop fusion | flops 785920 | bytes 1574912 | tf_op jit(solution)/shard_map/reduce_sum | solution.py:26
  1.6 1.0 convert_reduce_fusion
  2.6 0.7 multiply_add_fusion
  3.3 2.6 %fusion.5 = bf16[1024,768]{1,0:T(8,128)(2,1)S(1)} fusion(s32[512]{0:T(512)S(1)} %multiply_add_fusion, f32[512,768]{1,0:T(8,128)} %param.3, f32[512]{0:T(512)S(1)} %add_rsqrt_fusion), kind=kOutput, calls=%fused_computation.12 | convolution fusion | flops 807403520 | bytes 3149824 | tf_op jit(solution)/shard_map/dot_general | solution.py:33
  5.9 43.2 %all_to_all.20 = bf16[16,64,768]{2,1,0:T(8,128)(2,1)S(1)} all-to-all(bf16[16,64,768]{2,1,0:T(8,128)(2,1)S(1)} %bitcast.18), channel_id=1, replica_groups=mesh['parts'=2,'blk'=16] {'blk'}, dimensions={0} | all-to-all | bytes 3145728 | tf_op jit(solution)/shard_map/all_to_all | solution.py:44
  49.1 0.0 copy-start
  49.1 0.8 collective-permute-start.1
  49.9 3.0 %collective-permute-done.1 = bf16[1024,768]{1,0:T(8,128)(2,1)S(1)} collective-permute-done((bf16[1024,768]{1,0:T(8,128)(2,1)S(1)}, bf16[1024,768]{1,0:T(8,128)(2,1)S(1)}, u32[]{:S(2)}, u32[]{:S(2)}) %collective-permute-start.1) | collective-permute-done | bytes 1572896 | tf_op jit(solution)/shard_map/ppermute | solution.py:10
  52.9 1.9 %pad_maximum_fusion = bf16[2048,768]{1,0:T(8,128)(2,1)} fusion(bf16[1024,768]{1,0:T(8,128)(2,1)S(1)} %collective-permute-done.1, bf16[1024,768]{1,0:T(8,128)(2,1)S(1)} %bitcast.14), kind=kLoop, calls=%fused_computation.6 | loop fusion | flops 6291456 | bytes 6291456 | tf_op jit(solution)/shard_map/concatenate | solution.py:62
  54.8 1.3 collective-permute-start.3
  56.1 0.0 copy-done
  56.1 1.0 fusion.4
  57.1 0.1 all_to_all.13
  57.2 68.4 %all_to_all.21 = s32[16,1,64]{2,1,0:T(1,128)S(1)} all-to-all(s32[16,1,64]{2,1,0:T(1,128)S(1)} %all_to_all.13), channel_id=1, replica_groups=mesh['parts'=2,'blk'=16] {'blk'}, dimensions={0} | all-to-all | bytes 8192 | tf_op jit(solution)/shard_map/all_to_all | solution.py:51
  125.6 0.5 broadcast.48
  126.1 0.7 reduce.6
  126.8 0.1 eq.94
  126.8 0.1 collective-permute-start
  126.9 1.1 collective-permute-done
  128.0 1.3 collective-permute-start.2
  129.3 2.4 %collective-permute-done.2 = s32[2048]{0:T(1024)S(1)} collective-permute-done((s32[2048]{0:T(1024)S(1)}, s32[2048]{0:T(1024)S(1)}, u32[]{:S(2)}, u32[]{:S(2)}) %collective-permute-start.2) | collective-permute-done | bytes 8224 | tf_op jit(solution)/shard_map/ppermute | solution.py:10
  131.7 2.8 %select_reduce_fusion.2 = f32[1024]{0:T(1024)S(1)} fusion(s32[1024]{0:T(1024)S(1)} %eq.94, pred[1024]{0:T(1024)(128)(4,1)S(1)} %broadcast_compare_fusion.2, bf16[1024,768]{1,0:T(8,128)(2,1)S(1)} %bitcast.15), kind=kOutput, calls=%fused_computation.2 | convolution fusion | flops 1617951744 | bytes 1582080 | tf_op jit(solution)/shard_map/qd,kd->qk/dot_general | solution.py:14
  134.5 2.3 %select_reduce_fusion.1 = f32[1024]{0:T(1024)S(1)} fusion(s32[1024]{0:T(1024)S(1)} %eq.94, s32[1024]{0:T(1024)S(1)} %collective-permute-done, pred[1024]{0:T(1024)(128)(4,1)S(1)} %broadcast_compare_fusion.1, bf16[1024,768]{1,0:T(8,128)(2,1)S(1)} %bitcast.16, bf16[1024,768]{1,0:T(8,128)(2,1)S(1)} %collective-permute-done.1), kind=kOutput, calls=%fused_computation.1 | convolution fusion | flops 1614806016 | bytes 3159040 | tf_op jit(solution)/shard_map/qd,kd->qk/dot_general | solution.py:14
  136.8 0.0 collective-permute-done.3
  136.8 5.9 %select_reduce_fusion = f32[1024]{0:T(1024)S(1)} fusion(s32[2048]{0:T(1024)S(1)} %collective-permute-done.2, s32[1024]{0:T(1024)S(1)} %eq.94, pred[2048]{0:T(1024)(128)(4,1)S(1)} %broadcast_compare_fusion, bf16[1024,768]{1,0:T(8,128)(2,1)S(1)} %bitcast.17, bf16[2048,768]{1,0:T(8,128)(2,1)} %collective-permute-done.3), kind=kOutput, calls=%fused_computation | convolution fusion | flops 3229613056 | bytes 4737024 | tf_op jit(solution)/shard_map/qd,kd->qk/dot_general | solution.py:14
  142.7 0.1 max.28
  142.8 10.8 %all_to_all.22 = f32[16,1,64]{2,1,0:T(1,128)S(1)} all-to-all(f32[16,1,64]{2,1,0:T(1,128)S(1)} %max.28), channel_id=1, replica_groups=mesh['parts'=2,'blk'=16] {'blk'}, dimensions={0} | all-to-all | bytes 8192 | tf_op jit(solution)/shard_map/all_to_all | solution.py:64
  153.6 0.5 broadcast.49
  154.1 0.7 reduce.7
  154.8 0.1 reshape.88
  154.8 1.7 %fusion.2 = f32[1,512]{1,0:T(1,128)} fusion(f32[1024,1]{0,1:T(1,128)S(1)} %reshape.88, s32[512]{0:T(512)S(1)} %multiply_add_fusion), kind=kOutput, calls=%fused_computation.9 | convolution fusion | flops 6815744 | bytes 8192 | tf_op jit(solution)/shard_map/dot_general | solution.py:67
  (8 shorter events, 0.0 us)
Async XLA Ops:
  49.1 7.0 %copy-start = (s32[512]{0:T(512)S(1)}, s32[512]{0:T(512)}, u32[]{:S(2)}) copy-start(s32[512]{0:T(512)} %param.5) | copy-start | bytes 6148
  49.1 3.8 %collective-permute-start.1 = (bf16[1024,768]{1,0:T(8,128)(2,1)S(1)}, bf16[1024,768]{1,0:T(8,128)(2,1)S(1)}, u32[]{:S(2)}, u32[]{:S(2)}) collective-permute-start(bf16[1024,768]{1,0:T(8,128)(2,1)S(1)} %bitcast.13), channel_id=1, source_target_pairs={{0,1},{1,0},{2,3},{3,2},{4,5},{5,4},{6,7},{7,6},{8,9},{9,8},{10,11... | collective-permute-start | bytes 4718600 | tf_op jit(solution)/shard_map/ppermute | solution.py:10
  54.8 82.0 %collective-permute-start.3 = (bf16[2048,768]{1,0:T(8,128)(2,1)}, bf16[2048,768]{1,0:T(8,128)(2,1)}, u32[]{:S(2)}, u32[]{:S(2)}) collective-permute-start(bf16[2048,768]{1,0:T(8,128)(2,1)} %pad_maximum_fusion), channel_id=1, source_target_pairs={{0,2},{1,3},{2,0},{3,1},{4,6},{5,7},{6,4},{7,5},{8,10},{9,11},{10,... | collective-permute-start | bytes 9437192 | tf_op jit(solution)/shard_map/ppermute | solution.py:10
  126.8 1.2 collective-permute-start
  128.0 3.7 %collective-permute-start.2 = (s32[2048]{0:T(1024)S(1)}, s32[2048]{0:T(1024)S(1)}, u32[]{:S(2)}, u32[]{:S(2)}) collective-permute-start(s32[2048]{0:T(1024)S(1)} %pad_add_fusion), channel_id=1, source_target_pairs={{0,2},{1,3},{2,0},{3,1},{4,6},{5,7},{6,4},{7,5},{8,10},{9,11},{10,... | collective-permute-start | bytes 24584 | tf_op jit(solution)/shard_map/ppermute | solution.py:10
where the time goes:
time: 157 us
  blocking collectives  122 us (78%)
  matrix products  16.3 us (10%)
  other arithmetic  6.53 us (4%)
  waiting for transfers between devices  6.48 us (4%)
  starting transfers between devices  3.42 us (2%)
    all_to_all x1, blocking collectives, on_device(): lax.all_to_all(send_label.reshape(devices, capacity), 'blk', split_axis=0...  68.4 us
    all_to_all x1, blocking collectives, on_device(): lax.all_to_all(send_vec.reshape(devices, capacity, width), 'blk', split_a...  43.2 us
    dot_general x3, matrix products, compare(): jnp.einsum('qd,kd->qk', q_vec, k_vec, preferred_element_type=jnp.float32)  11 us
    all_to_all x1, blocking collectives, on_device(): lax.all_to_all(best.reshape(devices, capacity), 'blk', split_axis=0, conc...  10.8 us
    ppermute x4, waiting for transfers between devices, from_partner(): lax.ppermute(array, axis, [(i, i ^ 1 << distance) for i in range(lax.axis...  6.48 us
    ppermute x4, starting transfers between devices, from_partner(): lax.ppermute(array, axis, [(i, i ^ 1 << distance) for i in range(lax.axis...  3.42 us
  transfers between devices with their start and end apart: 4, of which 3 were waited for; matrix products, arithmetic and copies ran while one was open for 5% of the time, Pallas kernels for 0%

commit v1 on v0

v1 whole, which is shorter than its diff:
```python
import jax
import jax.numpy as jnp
from jax import lax
from jax.experimental import pallas as pl
from jax.experimental.pallas import tpu as pltpu
from jax.sharding import PartitionSpec as P

GROUP = 4
STAGES = 4
NT = (((1,), (1,)), ((), ()))


def iota(shape, axis):
    return lax.broadcasted_iota(jnp.int32, shape, axis)


def pack_kernel(groups, cap, emb_ref, owner_ref, cluster_ref, *outs):
    blocks, label_ref, slot_ref = outs[:STAGES], outs[STAGES], outs[STAGES + 1]
    rows = emb_ref.shape[0]
    x = emb_ref[...]
    squares = jnp.sum(x * x, axis=1, keepdims=True)
    unit = (x * lax.rsqrt(squares + 1e-06)).astype(jnp.bfloat16)
    mine = lax.axis_index("blk") // GROUP
    rel = (owner_ref[...] >> 2) ^ mine
    tall = max(groups, 16)
    member = iota((tall, rows), 0) == rel
    earlier = (iota((rows, rows), 0) < iota((rows, rows), 1)).astype(jnp.bfloat16)
    count = jnp.dot(member.astype(jnp.bfloat16), earlier, preferred_element_type=jnp.float32)
    rank = jnp.sum(jnp.where(member, count, 0.0), axis=0, keepdims=True)
    slot = rel * cap + rank.astype(jnp.int32)
    slot_ref[...] = slot
    label = ((cluster_ref[...] & 15) + 1).astype(jnp.float32).astype(jnp.bfloat16)
    label = jnp.broadcast_to(label, (16, rows))
    size = groups * cap // STAGES
    for s in range(STAGES):
        hot = (iota((size, rows), 0) + s * size == slot).astype(jnp.bfloat16)
        blocks[s][...] = jnp.dot(hot, unit, preferred_element_type=jnp.float32).astype(jnp.bfloat16)
        packed = lax.dot_general(label, hot, NT, preferred_element_type=jnp.float32)
        label_ref[:, s * size : (s + 1) * size] = packed[0:1, :] - 1.0


def pack(groups, cap, embedding, owner, cluster):
    rows, width = embedding.shape
    size = groups * cap // STAGES
    block = jax.ShapeDtypeStruct((size, width), jnp.bfloat16)
    return pl.pallas_call(
        lambda *refs: pack_kernel(groups, cap, *refs),
        out_shape=[block] * STAGES
        + [
            jax.ShapeDtypeStruct((1, groups * cap), jnp.float32),
            jax.ShapeDtypeStruct((1, rows), jnp.int32),
        ],
        compiler_params=pltpu.CompilerParams(vmem_limit_bytes=48 << 20),
        name="pack",
    )(embedding, owner.reshape(1, rows), cluster.reshape(1, rows))


def compare_kernel(stage, labels_ref, *refs):
    keys, best_ref, out_ref = refs[: 4 * stage + 4], refs[4 * stage + 4], refs[-1]
    size = keys[0].shape[0]

    def tile(q, k, peer, best):
        scores = lax.dot_general(
            keys[4 * k + peer][...], keys[4 * q][...], NT, preferred_element_type=jnp.float32
        )
        mine = labels_ref[0:1, q * size : (q + 1) * size]
        allowed = columns[k][:, peer : peer + 1] == mine
        if peer == 0 and q == k:
            allowed = allowed & (iota((size, size), 0) != iota((size, size), 1))
        return jnp.maximum(best, jnp.max(jnp.where(allowed, scores, -1.0), axis=0, keepdims=True))

    columns = [labels_ref[:, k * size : (k + 1) * size].T for k in range(stage + 1)]
    for q in range(stage + 1):
        if q < stage:
            best = best_ref[:, q * size : (q + 1) * size]
        else:
            best = jnp.full((1, size), -1.0, jnp.float32)
        for k in range(stage + 1) if q == stage else [stage]:
            for peer in range(4):
                best = tile(q, k, peer, best)
        out_ref[:, q * size : (q + 1) * size] = best


def compare(stage, labels, keys, best):
    size, width = keys[0].shape
    tiles = 8 * stage + 4
    return pl.pallas_call(
        lambda *refs: compare_kernel(stage, *refs),
        out_shape=jax.ShapeDtypeStruct((1, (stage + 1) * size), jnp.float32),
        compiler_params=pltpu.CompilerParams(vmem_limit_bytes=48 << 20),
        cost_estimate=pl.CostEstimate(
            flops=2 * tiles * size * size * width,
            bytes_accessed=len(keys) * size * width * 2,
            transcendentals=0,
        ),
        name=f"compare{stage}",
    )(labels, *keys, best)


def unpack_kernel(slot_ref, *refs):
    out_ref = refs[-1]
    slot = slot_ref[...]
    rows = slot.shape[1]
    total = jnp.zeros((8, rows), jnp.float32)
    start = 0
    for ref in refs[:-1]:
        size = ref.shape[1]
        column = jnp.broadcast_to(ref[...], (8, size)).T[:, 0:1]
        hit = iota((size, rows), 0) + start == slot
        part = jnp.where(hit, column, 0.0)
        total = total + jnp.sum(part.reshape(size // 8, 8, rows), axis=0)
        start += size
    out_ref[...] = jnp.sum(total, axis=0, keepdims=True)


def unpack(slot, backs):
    return pl.pallas_call(
        unpack_kernel,
        out_shape=jax.ShapeDtypeStruct(slot.shape, jnp.float32),
        name="unpack",
    )(slot, *backs)


def on_device(embedding, row_owner, cluster_id):
    rows, _ = embedding.shape
    devices = lax.axis_size("blk")
    groups = devices // GROUP
    cap = GROUP * max(2, 2 * rows // devices)
    size = groups * cap // STAGES
    per_stage = groups // STAGES

    def swap(array, mask):
        return lax.ppermute(array, "blk", [(i, i ^ mask) for i in range(devices)])

    sends = pack(groups, cap, embedding, row_owner, cluster_id)
    blocks, label, slot = sends[:STAGES], sends[STAGES], sends[STAGES + 1]
    every = lax.all_gather(label.reshape(groups * cap), "blk").reshape(devices, groups, cap)
    mine = lax.axis_index("blk")
    steps = jnp.arange(groups)
    sources = (mine ^ jnp.arange(4)[:, None]) ^ (steps[None, :] * GROUP)
    labels = every[sources, steps[None, :]].reshape(4, groups * cap)
    labels = jnp.concatenate([labels, labels], axis=0)

    keys, best = [], jnp.full((1, 128), -1.0, jnp.float32)
    for s in range(STAGES):
        pieces = []
        for d in range(s * per_stage, (s + 1) * per_stage):
            piece = blocks[s][(d - s * per_stage) * cap : (d - s * per_stage + 1) * cap]
            pieces.append(swap(piece, d * GROUP) if d else piece)
        own = pieces[0] if per_stage == 1 else jnp.concatenate(pieces, axis=0)
        across = swap(own, 2)
        keys += [own, swap(own, 1), across, swap(across, 1)]
        best = compare(s, labels, keys, best)
    backs = []
    for d in range(groups):
        back = best[:, d * cap : (d + 1) * cap]
        backs.append(swap(back, d * GROUP) if d else back)
    if per_stage > 1:
        backs = [
            jnp.concatenate(backs[s * per_stage : (s + 1) * per_stage], axis=1)
            for s in range(STAGES)
        ]
    return unpack(slot, backs).reshape(rows)


def solution(mesh):
    placed = (P(("parts", "blk"), None), P(("parts", "blk")), P(("parts", "blk")))
    return jax.shard_map(
        on_device, mesh=mesh, in_specs=placed, out_specs=P(("parts", "blk")), check_vma=False
    )
```

time: 157 us -> 98.1 us (0.62)
  blocking collectives: 122 us -> 28.3 us
  waiting for transfers between devices: 6.48 us -> 26.4 us
  matrix products: 16.3 us -> 0 us
  Pallas kernels: 0 us -> 14.8 us
  starting transfers between devices: 3.42 us -> 17.3 us
  local copies, waits for them, and re-layouts: 1.33 us -> 9 us
  other arithmetic: 6.53 us -> 1.7 us
    all_to_all x3 -> x0, blocking collectives: 122 us -> none  [the longest x1 68.4 us: on_device(): lax.all_to_all(send_label.reshape(devices, capacity), 'blk', split_axis=0...]
    all_gather x0 -> x1, blocking collectives: none -> 28.3 us  [on_device(): lax.all_gather(label.reshape(groups * cap), 'blk')]
    ppermute x4 -> x18, waiting for transfers between devices: 6.48 us -> 26.4 us  [swap(): return lax.ppermute(array, 'blk', [(i, i ^ mask) for i in range(devices)])]
    dot_general x6 -> x0, matrix products: 16.3 us -> none  [the longest x3 11 us: compare(): jnp.einsum('qd,kd->qk', q_vec, k_vec, preferred_element_type=jnp.float32)]
    pallas_call x0 -> x6, Pallas kernels: none -> 14.8 us  [the longest x4 11.6 us: compare(): pl.pallas_call(lambda *refs: compare_kernel(stage, *refs), out_shape=jax....]
    ppermute x4 -> x18, starting transfers between devices: 3.42 us -> 17.3 us  [swap(): return lax.ppermute(array, 'blk', [(i, i ^ mask) for i in range(devices)])]
    unnamed x2 -> x16, local copies, waits for them, and re-layouts: 0.01 us -> 4.08 us
    reduce_sum x2 -> x0, other arithmetic: 2.59 us -> none  [the longest x1 1.58 us: on_device(): squares = jnp.sum(embedding * embedding, axis=1, keepdims=True)]
  transfers between devices with their start and end apart: 4 -> 18, of which waited for: 3 -> 4; matrix products, arithmetic and copies ran while one was open for 5% -> 6% of each run, Pallas kernels for 0% -> 7%
where the time goes in v1:
time: 98.1 us; the launch traced here: 97.6 us
  blocking collectives  28.3 us (29%)
  waiting for transfers between devices  26.4 us (27%)
  starting transfers between devices  17.3 us (18%)
  Pallas kernels  14.8 us (15%)
  local copies, waits for them, and re-layouts  9 us (9%)
  other arithmetic  1.7 us (2%)
    all_gather x1, blocking collectives, on_device(): lax.all_gather(label.reshape(groups * cap), 'blk')  28.3 us
    ppermute x18, waiting for transfers between devices, swap(): return lax.ppermute(array, 'blk', [(i, i ^ mask) for i in range(devices)])  26.4 us
    ppermute x18, starting transfers between devices, swap(): return lax.ppermute(array, 'blk', [(i, i ^ mask) for i in range(devices)])  17.3 us
    pallas_call x4, Pallas kernels, compare(): pl.pallas_call(lambda *refs: compare_kernel(stage, *refs), out_shape=jax....  11.6 us
    unnamed x16, local copies, waits for them, and re-layouts  4.08 us
    gather x1, local copies, waits for them, and re-layouts, on_device(): labels = every[sources, steps[None, :]].reshape(4, groups * cap)  2.03 us
  transfers between devices with their start and end apart: 18, of which 4 were waited for; matrix products, arithmetic and copies ran while one was open for 6% of the time, Pallas kernels for 7%

profile of v1, /device:TPU:0, one launch (start us, length us, event | category | flops | bytes accessed | tf_op | source)
XLA Modules:
  0.0 97.6 jit_solution(15805788190079834962)
XLA Ops:
  0.0 0.0 copy-start
  0.0 1.4 %copy-done = f32[512,768]{1,0:T(8,128)S(1)} copy-done((f32[512,768]{1,0:T(8,128)S(1)}, f32[512,768]{1,0:T(8,128)}, u32[]{:S(2)}) %copy-start) | copy-done | bytes 1572888
  1.4 0.0 copy-start.1
  1.4 0.7 copy-done.1
  2.1 0.0 copy-start.2
  2.1 0.7 copy-done.2
  2.8 1.4 %pack.1 = (bf16[256,768]{1,0:T(8,128)(2,1)S(1)}, bf16[256,768]{1,0:T(8,128)(2,1)S(1)}, bf16[256,768]{1,0:T(8,128)(2,1)S(1)}, bf16[256,768]{1,0:T(8,128)(2,1)S(1)...) custom-call(f32[512,768]{1,0:T(8,128)S(1)} %copy-done, s32[1,512]{1,0:T(1,128)S(1)} %bitcast.7, s32[1,512]{1,0:T(1,128)S(1)} %bitcast.8), custom_call_target="tpu_custom_call" | custom-call | tf_op jit(solution)/shard_map/pack/pallas_call | solution.py:46
  4.2 0.0 copy-start.3
  4.2 3.1 %collective-permute-start.3 = (bf16[256,768]{1,0:T(8,128)(2,1)S(1)}, bf16[256,768]{1,0:T(8,128)(2,1)S(1)}, u32[]{:S(2)}, u32[]{:S(2)}) collective-permute-start(bf16[256,768]{1,0:T(8,128)(2,1)S(1)} %get-tuple-element.14), channel_id=1, source_target_pairs={{0,4},{1,5},{2,6},{3,7},{4,0},{5,1},{6,2},{7,3},{8,12},{9,13},{10,... | collective-permute-start | bytes 1179656 | tf_op jit(solution)/shard_map/ppermute | solution.py:133
  7.3 1.5 %collective-permute-start.1 = (bf16[256,768]{1,0:T(8,128)(2,1)S(1)}, bf16[256,768]{1,0:T(8,128)(2,1)S(1)}, u32[]{:S(2)}, u32[]{:S(2)}) collective-permute-start(bf16[256,768]{1,0:T(8,128)(2,1)S(1)} %get-tuple-element.13.refs_1_), channel_id=1, source_target_pairs={{0,2},{1,3},{2,0},{3,1},{4,6},{5,7},{6,4},{7,5},{8,10},{9,11},{10,... | collective-permute-start | bytes 1179656 | tf_op jit(solution)/shard_map/ppermute | solution.py:133
  8.8 2.6 %collective-permute-start.7 = (bf16[256,768]{1,0:T(8,128)(2,1)S(1)}, bf16[256,768]{1,0:T(8,128)(2,1)S(1)}, u32[]{:S(2)}, u32[]{:S(2)}) collective-permute-start(bf16[256,768]{1,0:T(8,128)(2,1)S(1)} %get-tuple-element.15), channel_id=1, source_target_pairs={{0,8},{1,9},{2,10},{3,11},{4,12},{5,13},{6,14},{7,15},{8,0},{9,1},... | collective-permute-start | bytes 1179656 | tf_op jit(solution)/shard_map/ppermute | solution.py:133
  11.4 0.0 collective-permute-start
  11.4 0.2 collective-permute-start.11
  11.6 11.7 %collective-permute-done.3.refs_5_ = bf16[256,768]{1,0:T(8,128)(2,1)S(1)} collective-permute-done((bf16[256,768]{1,0:T(8,128)(2,1)S(1)}, bf16[256,768]{1,0:T(8,128)(2,1)S(1)}, u32[]{:S(2)}, u32[]{:S(2)}) %collective-permute-start.3) | collective-permute-done | bytes 393248 | tf_op jit(solution)/shard_map/ppermute | solution.py:133
  23.3 2.1 %collective-permute-start.5 = (bf16[256,768]{1,0:T(8,128)(2,1)S(1)}, bf16[256,768]{1,0:T(8,128)(2,1)S(1)}, u32[]{:S(2)}, u32[]{:S(2)}) collective-permute-start(bf16[256,768]{1,0:T(8,128)(2,1)S(1)} %collective-permute-done.3.refs_5_), channel_id=1, source_target_pairs={{0,2},{1,3},{2,0},{3,1},{4,6},{5,7},{6,4},{7,5},{8,10},{9,11},{10,... | collective-permute-start | bytes 1179656 | tf_op jit(solution)/shard_map/ppermute | solution.py:133
  25.5 0.0 collective-permute-done.1.refs_3_
  25.5 0.0 collective-permute-start.2
  25.5 13.1 %collective-permute-done.7.refs_9_ = bf16[256,768]{1,0:T(8,128)(2,1)S(1)} collective-permute-done((bf16[256,768]{1,0:T(8,128)(2,1)S(1)}, bf16[256,768]{1,0:T(8,128)(2,1)S(1)}, u32[]{:S(2)}, u32[]{:S(2)}) %collective-permute-start.7) | collective-permute-done | bytes 393248 | tf_op jit(solution)/shard_map/ppermute | solution.py:133
  38.6 0.5 collective-permute-start.9
  39.2 0.0 collective-permute-done.refs_2_
  39.2 0.0 copy-done.3
  39.2 0.0 collective-permute-start.4
  39.2 0.0 collective-permute-done.11.refs_13_
  39.2 1.6 %collective-permute-start.13 = (bf16[256,768]{1,0:T(8,128)(2,1)S(1)}, bf16[256,768]{1,0:T(8,128)(2,1)}, u32[]{:S(2)}, u32[]{:S(2)}) collective-permute-start(bf16[256,768]{1,0:T(8,128)(2,1)S(1)} %collective-permute-done.11.refs_13_), channel_id=1, source_target_pairs={{0,2},{1,3},{2,0},{3,1},{4,6},{5,7},{6,4},{7,5},{8,10},{9,11},{10,... | collective-permute-start | bytes 1179656 | tf_op jit(solution)/shard_map/ppermute | solution.py:133
  40.7 0.0 collective-permute-done.5.refs_7_
  40.7 0.2 collective-permute-start.6
  40.9 28.3 %all-gather = f32[16,1,1024]{2,1,0:T(1,128)} all-gather(f32[1,1,1024]{2,1,0:T(1,128)S(1)} %bitcast.6), channel_id=1, replica_groups=mesh['parts'=2,'blk'=16] {'blk'}, dimensions={0}, use_global_device_ids=true | all-gather | bytes 69632 | tf_op jit(solution)/shard_map/all_gather | solution.py:137
  69.2 1.6 %reduce = f32[16,1024]{1,0:T(8,128)} reduce(f32[16,1,1024]{2,1,0:T(1,128)} %all-gather, f32[]{:T(128)} %constant.27), dimensions={1}, to_apply=%all-gather.reduce_sub_computation | reduce | bytes 131076 | tf_op jit(solution)/shard_map/all_gather | solution.py:137
  70.8 1.5 %reshape.82 = f32[16,4,256]{2,1,0:T(4,128)} reshape(f32[16,1024]{1,0:T(8,128)} %reduce) | data formatting | bytes 131072 | tf_op jit(solution)/shard_map/reshape | solution.py:137
  72.3 0.0 collective-permute-done.2.refs_4_
  72.3 0.3 collective-permute-start.8
  72.7 0.0 collective-permute-done.9.refs_11_
  72.7 0.2 collective-permute-start.10
  72.9 0.1 fusion.2
  72.9 0.1 reshape.85
  73.0 2.0 %gather_fusion = f32[16,256]{1,0:T(8,128)} fusion(f32[16,4,256]{2,1,0:T(4,128)} %reshape.82, s32[16]{0:T(128)S(1)} %reshape.85), kind=kCustom, calls=%fused_computation | custom fusion | bytes 32896 | tf_op jit(solution)/shard_map/gather | solution.py:141
  75.0 0.7 reshape.83
  75.8 0.0 collective-permute-done.4.refs_6_
  75.8 0.4 collective-permute-start.12
  76.2 0.0 collective-permute-done.13.refs_15_
  76.2 0.2 collective-permute-start.14
  76.4 0.6 compare0.1.refs_9_
  77.0 0.0 collective-permute-done.6.refs_8_
  77.0 2.6 %compare1.1.refs_13_ = f32[1,512]{1,0:T(1,128)S(1)} custom-call(f32[8,1024]{1,0:T(8,128)S(1)} %pad_maximum_fusion.refs_0_, bf16[256,768]{1,0:T(8,128)(2,1)S(1)} %get-tuple-element.13.refs_1_, bf16[256,768]{1,0:T(8,128)(2,1)S(1)} %collective-permute-done.refs_2_, bf16[256,768]{1,0:T(8,128)(2,1)S(1)} %collective-permute-done.1.refs_3_, ...), custom_call_target="tpu_custom_call" | custom-call | flops 1207959552 | bytes 3145728 | tf_op jit(solution)/shard_map/compare1/pallas_call | solution.py:87
  79.6 0.0 collective-permute-done.8.refs_10_
  79.6 0.0 collective-permute-done.10.refs_12_
  79.6 3.6 %compare2.1.refs_17_ = f32[1,768]{1,0:T(1,128)S(1)} custom-call(f32[8,1024]{1,0:T(8,128)S(1)} %pad_maximum_fusion.refs_0_, bf16[256,768]{1,0:T(8,128)(2,1)S(1)} %get-tuple-element.13.refs_1_, bf16[256,768]{1,0:T(8,128)(2,1)S(1)} %collective-permute-done.refs_2_, bf16[256,768]{1,0:T(8,128)(2,1)S(1)} %collective-permute-done.1.refs_3_, ...), custom_call_target="tpu_custom_call" | custom-call | flops 2013265920 | bytes 4718592 | tf_op jit(solution)/shard_map/compare2/pallas_call | solution.py:87
  83.3 0.0 collective-permute-done.12.refs_14_
  83.3 0.0 collective-permute-done.14.refs_16_
  83.3 0.0 copy-start.7
  83.3 0.7 copy-done.7
  84.0 4.7 %compare3.1 = f32[1,1024]{1,0:T(1,128)S(1)} custom-call(f32[8,1024]{1,0:T(8,128)S(1)} %pad_maximum_fusion.refs_0_, bf16[256,768]{1,0:T(8,128)(2,1)S(1)} %get-tuple-element.13.refs_1_, bf16[256,768]{1,0:T(8,128)(2,1)S(1)} %collective-permute-done.refs_2_, bf16[256,768]{1,0:T(8,128)(2,1)S(1)} %collective-permute-done.1.refs_3_, ...), custom_call_target="tpu_custom_call" | custom-call | flops 2818572288 | bytes 6291456 | tf_op jit(solution)/shard_map/compare3/pallas_call | solution.py:87
  88.8 0.6 fusion.3
  89.4 0.0 collective-permute-start.15
  89.4 0.0 collective-permute-start.16
  89.4 4.4 %collective-permute-start.17 = (f32[1,256]{1,0:T(1,128)S(1)}, f32[1,256]{1,0:T(1,128)S(1)}, u32[]{:S(2)}, u32[]{:S(2)}) collective-permute-start(f32[1,256]{1,0:T(1,128)S(1)} %get-tuple-element.17), channel_id=1, source_target_pairs={{0,12},{1,13},{2,14},{3,15},{4,8},{5,9},{6,10},{7,11},{8,4},{9,5},... | collective-permute-start | bytes 3080 | tf_op jit(solution)/shard_map/ppermute | solution.py:133
  93.7 0.0 collective-permute-done.15.refs_1_
  93.7 0.0 copy-start.4
  93.7 0.1 collective-permute-done.16.refs_2_
  93.8 1.5 %collective-permute-done.17.refs_3_ = f32[1,256]{1,0:T(1,128)S(1)} collective-permute-done((f32[1,256]{1,0:T(1,128)S(1)}, f32[1,256]{1,0:T(1,128)S(1)}, u32[]{:S(2)}, u32[]{:S(2)}) %collective-permute-start.17) | collective-permute-done | bytes 1056 | tf_op jit(solution)/shard_map/ppermute | solution.py:133
  95.3 0.0 copy-done.4
  95.3 0.0 copy-done.5
  95.3 0.6 copy-done.6
  95.9 1.8 %unpack.1 = f32[1,512]{1,0:T(1,128)} custom-call(s32[1,512]{1,0:T(1,128)} %copy-done.3, f32[1,256]{1,0:T(1,128)} %get-tuple-element.20.refs_0_, f32[1,256]{1,0:T(1,128)} %copy-done.4, f32[1,256]{1,0:T(1,128)} %copy-done.5, f32[1,256]{1,0:T(1,128)} %copy-done.6), custom_call_target="tpu_custom_call" | custom-call | tf_op jit(solution)/shard_map/unpack/pallas_call | solution.py:117
  (5 shorter events, 0.0 us)
Async XLA Ops:
  0.0 1.4 %copy-start = (f32[512,768]{1,0:T(8,128)S(1)}, f32[512,768]{1,0:T(8,128)}, u32[]{:S(2)}) copy-start(f32[512,768]{1,0:T(8,128)} %refs_0_.1) | copy-start | bytes 4718596
  1.4 0.7 copy-start.1
  2.1 0.7 copy-start.2
  4.2 34.9 %copy-start.3 = (s32[1,512]{1,0:T(1,128)}, s32[1,512]{1,0:T(1,128)S(1)}, u32[]{:S(2)}) copy-start(s32[1,512]{1,0:T(1,128)S(1)} %get-tuple-element.11.slot_ref) | copy-start | bytes 6148
  4.2 19.1 %collective-permute-start.3 = (bf16[256,768]{1,0:T(8,128)(2,1)S(1)}, bf16[256,768]{1,0:T(8,128)(2,1)S(1)}, u32[]{:S(2)}, u32[]{:S(2)}) collective-permute-start(bf16[256,768]{1,0:T(8,128)(2,1)S(1)} %get-tuple-element.14), channel_id=1, source_target_pairs={{0,4},{1,5},{2,6},{3,7},{4,0},{5,1},{6,2},{7,3},{8,12},{9,13},{10,... | collective-permute-start | bytes 1179656 | tf_op jit(solution)/shard_map/ppermute | solution.py:133
  7.3 18.2 %collective-permute-start.1 = (bf16[256,768]{1,0:T(8,128)(2,1)S(1)}, bf16[256,768]{1,0:T(8,128)(2,1)S(1)}, u32[]{:S(2)}, u32[]{:S(2)}) collective-permute-start(bf16[256,768]{1,0:T(8,128)(2,1)S(1)} %get-tuple-element.13.refs_1_), channel_id=1, source_target_pairs={{0,2},{1,3},{2,0},{3,1},{4,6},{5,7},{6,4},{7,5},{8,10},{9,11},{10,... | collective-permute-start | bytes 1179656 | tf_op jit(solution)/shard_map/ppermute | solution.py:133
  8.8 29.8 %collective-permute-start.7 = (bf16[256,768]{1,0:T(8,128)(2,1)S(1)}, bf16[256,768]{1,0:T(8,128)(2,1)S(1)}, u32[]{:S(2)}, u32[]{:S(2)}) collective-permute-start(bf16[256,768]{1,0:T(8,128)(2,1)S(1)} %get-tuple-element.15), channel_id=1, source_target_pairs={{0,8},{1,9},{2,10},{3,11},{4,12},{5,13},{6,14},{7,15},{8,0},{9,1},... | collective-permute-start | bytes 1179656 | tf_op jit(solution)/shard_map/ppermute | solution.py:133
  11.4 27.8 %collective-permute-start = (bf16[256,768]{1,0:T(8,128)(2,1)S(1)}, bf16[256,768]{1,0:T(8,128)(2,1)S(1)}, u32[]{:S(2)}, u32[]{:S(2)}) collective-permute-start(bf16[256,768]{1,0:T(8,128)(2,1)S(1)} %get-tuple-element.13.refs_1_), channel_id=1, source_target_pairs={{0,1},{1,0},{2,3},{3,2},{4,5},{5,4},{6,7},{7,6},{8,9},{9,8},{10,11... | collective-permute-start | bytes 1179656 | tf_op jit(solution)/shard_map/ppermute | solution.py:133
  11.4 27.8 %collective-permute-start.11 = (bf16[256,768]{1,0:T(8,128)(2,1)S(1)}, bf16[256,768]{1,0:T(8,128)(2,1)S(1)}, u32[]{:S(2)}, u32[]{:S(2)}) collective-permute-start(bf16[256,768]{1,0:T(8,128)(2,1)S(1)} %get-tuple-element.16), channel_id=1, source_target_pairs={{0,12},{1,13},{2,14},{3,15},{4,8},{5,9},{6,10},{7,11},{8,4},{9,5},... | collective-permute-start | bytes 1179656 | tf_op jit(solution)/shard_map/ppermute | solution.py:133
  23.3 17.4 %collective-permute-start.5 = (bf16[256,768]{1,0:T(8,128)(2,1)S(1)}, bf16[256,768]{1,0:T(8,128)(2,1)S(1)}, u32[]{:S(2)}, u32[]{:S(2)}) collective-permute-start(bf16[256,768]{1,0:T(8,128)(2,1)S(1)} %collective-permute-done.3.refs_5_), channel_id=1, source_target_pairs={{0,2},{1,3},{2,0},{3,1},{4,6},{5,7},{6,4},{7,5},{8,10},{9,11},{10,... | collective-permute-start | bytes 1179656 | tf_op jit(solution)/shard_map/ppermute | solution.py:133
  25.5 46.9 %collective-permute-start.2 = (bf16[256,768]{1,0:T(8,128)(2,1)S(1)}, bf16[256,768]{1,0:T(8,128)(2,1)S(1)}, u32[]{:S(2)}, u32[]{:S(2)}) collective-permute-start(bf16[256,768]{1,0:T(8,128)(2,1)S(1)} %collective-permute-done.1.refs_3_), channel_id=1, source_target_pairs={{0,1},{1,0},{2,3},{3,2},{4,5},{5,4},{6,7},{7,6},{8,9},{9,8},{10,11... | collective-permute-start | bytes 1179656 | tf_op jit(solution)/shard_map/ppermute | solution.py:133
  38.6 34.1 %collective-permute-start.9 = (bf16[256,768]{1,0:T(8,128)(2,1)S(1)}, bf16[256,768]{1,0:T(8,128)(2,1)S(1)}, u32[]{:S(2)}, u32[]{:S(2)}) collective-permute-start(bf16[256,768]{1,0:T(8,128)(2,1)S(1)} %collective-permute-done.7.refs_9_), channel_id=1, source_target_pairs={{0,2},{1,3},{2,0},{3,1},{4,6},{5,7},{6,4},{7,5},{8,10},{9,11},{10,... | collective-permute-start | bytes 1179656 | tf_op jit(solution)/shard_map/ppermute | solution.py:133
  39.2 36.6 %collective-permute-start.4 = (bf16[256,768]{1,0:T(8,128)(2,1)S(1)}, bf16[256,768]{1,0:T(8,128)(2,1)}, u32[]{:S(2)}, u32[]{:S(2)}) collective-permute-start(bf16[256,768]{1,0:T(8,128)(2,1)S(1)} %collective-permute-done.3.refs_5_), channel_id=1, source_target_pairs={{0,1},{1,0},{2,3},{3,2},{4,5},{5,4},{6,7},{7,6},{8,9},{9,8},{10,11... | collective-permute-start | bytes 1179656 | tf_op jit(solution)/shard_map/ppermute | solution.py:133
  39.2 37.0 %collective-permute-start.13 = (bf16[256,768]{1,0:T(8,128)(2,1)S(1)}, bf16[256,768]{1,0:T(8,128)(2,1)}, u32[]{:S(2)}, u32[]{:S(2)}) collective-permute-start(bf16[256,768]{1,0:T(8,128)(2,1)S(1)} %collective-permute-done.11.refs_13_), channel_id=1, source_target_pairs={{0,2},{1,3},{2,0},{3,1},{4,6},{5,7},{6,4},{7,5},{8,10},{9,11},{10,... | collective-permute-start | bytes 1179656 | tf_op jit(solution)/shard_map/ppermute | solution.py:133
  40.7 36.3 %collective-permute-start.6 = (bf16[256,768]{1,0:T(8,128)(2,1)S(1)}, bf16[256,768]{1,0:T(8,128)(2,1)}, u32[]{:S(2)}, u32[]{:S(2)}) collective-permute-start(bf16[256,768]{1,0:T(8,128)(2,1)S(1)} %collective-permute-done.5.refs_7_), channel_id=1, source_target_pairs={{0,1},{1,0},{2,3},{3,2},{4,5},{5,4},{6,7},{7,6},{8,9},{9,8},{10,11... | collective-permute-start | bytes 1179656 | tf_op jit(solution)/shard_map/ppermute | solution.py:133
  72.3 7.3 %collective-permute-start.8 = (bf16[256,768]{1,0:T(8,128)(2,1)S(1)}, bf16[256,768]{1,0:T(8,128)(2,1)}, u32[]{:S(2)}, u32[]{:S(2)}) collective-permute-start(bf16[256,768]{1,0:T(8,128)(2,1)S(1)} %collective-permute-done.7.refs_9_), channel_id=1, source_target_pairs={{0,1},{1,0},{2,3},{3,2},{4,5},{5,4},{6,7},{7,6},{8,9},{9,8},{10,11... | collective-permute-start | bytes 1179656 | tf_op jit(solution)/shard_map/ppermute | solution.py:133
  72.7 6.9 %collective-permute-start.10 = (bf16[256,768]{1,0:T(8,128)(2,1)S(1)}, bf16[256,768]{1,0:T(8,128)(2,1)}, u32[]{:S(2)}, u32[]{:S(2)}) collective-permute-start(bf16[256,768]{1,0:T(8,128)(2,1)S(1)} %collective-permute-done.9.refs_11_), channel_id=1, source_target_pairs={{0,1},{1,0},{2,3},{3,2},{4,5},{5,4},{6,7},{7,6},{8,9},{9,8},{10,11... | collective-permute-start | bytes 1179656 | tf_op jit(solution)/shard_map/ppermute | solution.py:133
  75.8 7.5 %collective-permute-start.12 = (bf16[256,768]{1,0:T(8,128)(2,1)S(1)}, bf16[256,768]{1,0:T(8,128)(2,1)S(1)}, u32[]{:S(2)}, u32[]{:S(2)}) collective-permute-start(bf16[256,768]{1,0:T(8,128)(2,1)S(1)} %collective-permute-done.11.refs_13_), channel_id=1, source_target_pairs={{0,1},{1,0},{2,3},{3,2},{4,5},{5,4},{6,7},{7,6},{8,9},{9,8},{10,11... | collective-permute-start | bytes 1179656 | tf_op jit(solution)/shard_map/ppermute | solution.py:133
  76.2 7.1 %collective-permute-start.14 = (bf16[256,768]{1,0:T(8,128)(2,1)}, bf16[256,768]{1,0:T(8,128)(2,1)S(1)}, u32[]{:S(2)}, u32[]{:S(2)}) collective-permute-start(bf16[256,768]{1,0:T(8,128)(2,1)} %collective-permute-done.13.refs_15_), channel_id=1, source_target_pairs={{0,1},{1,0},{2,3},{3,2},{4,5},{5,4},{6,7},{7,6},{8,9},{9,8},{10,11... | collective-permute-start | bytes 1179656 | tf_op jit(solution)/shard_map/ppermute | solution.py:133
  83.3 0.7 copy-start.7
  89.4 4.4 %collective-permute-start.15 = (f32[1,256]{1,0:T(1,128)S(1)}, f32[1,256]{1,0:T(1,128)S(1)}, u32[]{:S(2)}, u32[]{:S(2)}) collective-permute-start(f32[1,256]{1,0:T(1,128)S(1)} %get-tuple-element.19), channel_id=1, source_target_pairs={{0,4},{1,5},{2,6},{3,7},{4,0},{5,1},{6,2},{7,3},{8,12},{9,13},{10,... | collective-permute-start | bytes 3080 | tf_op jit(solution)/shard_map/ppermute | solution.py:133
  89.4 4.5 %collective-permute-start.16 = (f32[1,256]{1,0:T(1,128)S(1)}, f32[1,256]{1,0:T(1,128)S(1)}, u32[]{:S(2)}, u32[]{:S(2)}) collective-permute-start(f32[1,256]{1,0:T(1,128)S(1)} %get-tuple-element.18), channel_id=1, source_target_pairs={{0,8},{1,9},{2,10},{3,11},{4,12},{5,13},{6,14},{7,15},{8,0},{9,1},... | collective-permute-start | bytes 3080 | tf_op jit(solution)/shard_map/ppermute | solution.py:133
  89.4 5.9 %collective-permute-start.17 = (f32[1,256]{1,0:T(1,128)S(1)}, f32[1,256]{1,0:T(1,128)S(1)}, u32[]{:S(2)}, u32[]{:S(2)}) collective-permute-start(f32[1,256]{1,0:T(1,128)S(1)} %get-tuple-element.17), channel_id=1, source_target_pairs={{0,12},{1,13},{2,14},{3,15},{4,8},{5,9},{6,10},{7,11},{8,4},{9,5},... | collective-permute-start | bytes 3080 | tf_op jit(solution)/shard_map/ppermute | solution.py:133
  93.7 1.6 %copy-start.4 = (f32[1,256]{1,0:T(1,128)}, f32[1,256]{1,0:T(1,128)S(1)}, u32[]{:S(2)}) copy-start(f32[1,256]{1,0:T(1,128)S(1)} %collective-permute-done.15.refs_1_) | copy-start | bytes 3076
  93.8 1.5 %copy-start.5 = (f32[1,256]{1,0:T(1,128)}, f32[1,256]{1,0:T(1,128)S(1)}, u32[]{:S(2)}) copy-start(f32[1,256]{1,0:T(1,128)S(1)} %collective-permute-done.16.refs_2_) | copy-start | bytes 3076
  95.3 0.6 copy-start.6
